TPU v7x, 512 devices: a whole 4x4x16 slice. The times are simulated.
512 devices in a mesh: orient: 32 (over y_lo, z), brow: 2 (over core), bcol: 8 (over x, y_hi).
Axes of the slice: x: 4, y: 4 (y_hi: 2, y_lo: 2; y = y_hi * 2 + y_lo), z: 16, core: 2. Of those that a mesh axis runs over, the one named last changes fastest.
Arguments:
- volume: float32 [32, 64, 832], P('orient', 'brow', 'bcol'), may hold values from -700 to 700
- template: float32 [24, 24, 24], replicated, may hold values from 0 to 1
- voxel_maps: int32 [32, 13824], P('orient'), may hold values from 0 to 13823, as said below
Outputs:
- best: float32 [32, 64, 832], P('orient', 'brow', 'bcol')
Inputs may be any that keep to these rules, and one draw needn't show every extreme that they name: `voxel_maps`: each row holds every number of 0 to 13823 exactly once.
All inputs are finite; a program needn't handle non-finite values.
Results may differ from a plain program's by a relative error of at most 0.00013.
Values sent between devices are 32-bit elements; how exact they have to be, the bound alone decides.
No kernel may reach another device: no remote copies, remote signals or barrier semaphores. Data moves between devices by JAX's collectives and lax.ppermute only.
A program may use at most 64 MiB of HBM per device.

v0:
```python
import math
import jax
import jax.numpy as jnp
from jax import lax
from jax.sharding import PartitionSpec as P

epsilon = 1e-06
floor_share = 0.1
highest = lax.Precision.HIGHEST


def extended(cells, sides, width):
    for axis, dim in sides:
        count = lax.axis_size(axis)
        ends = count - 1
        head = lax.slice_in_dim(cells, 0, width, axis=dim)
        tail = lax.slice_in_dim(cells, cells.shape[dim] - width, cells.shape[dim], axis=dim)
        cells = jnp.concatenate(
            [
                lax.ppermute(tail, axis, [(i, (i + 1) % count) for i in range(ends)]),
                cells,
                lax.ppermute(head, axis, [((i + 1) % count, i) for i in range(ends)]),
            ],
            axis=dim,
        )
    return cells


def phase_tables(row_index, col_index, length):
    products = row_index[:, None] * col_index[None, :] % length
    angles = products.astype(jnp.float32) * (2.0 * math.pi / length)
    return (jnp.cos(angles), jnp.sin(angles))


def band_table(row_index, col_index, lower, upper):
    offsets = col_index[None, :] - row_index[:, None]
    return ((offsets >= lower) & (offsets < upper)).astype(jnp.float32)


def whiten_rows(rows_in):
    length = rows_in.shape[-1]
    frequency = jnp.arange(length, dtype=jnp.int32)
    cosine, sine_table = phase_tables(frequency, frequency, length)
    spec_real = jnp.dot(rows_in, cosine, precision=highest)
    spec_imag = -jnp.dot(rows_in, sine_table, precision=highest)
    power_spec = spec_real * spec_real + spec_imag * spec_imag
    smoothed = (
        jnp.roll(power_spec, 1, axis=1) + power_spec + jnp.roll(power_spec, -1, axis=1)
    ) / 3.0
    smoothed = smoothed + floor_share * jnp.mean(power_spec, axis=1, keepdims=True) + epsilon
    weights = lax.rsqrt(smoothed)
    whitened = jnp.dot(spec_real * weights, cosine, precision=highest) - jnp.dot(
        spec_imag * weights, sine_table, precision=highest
    )
    return whitened / math.sqrt(length)


def shards(volume, template, voxel_maps):
    plane_count, brick_rows, brick_cols = volume.shape
    template_edge = template.shape[0]
    half_edge = template_edge // 2
    depth_total = plane_count * lax.axis_size("orient")
    pad_rows = brick_rows + template_edge
    pad_cols = brick_cols + template_edge
    pad_depth = depth_total + template_edge
    pencils = lax.all_to_all(volume, "bcol", split_axis=1, concat_axis=2, tiled=True)
    whitened_rows = whiten_rows(pencils.reshape(-1, pencils.shape[-1])).reshape(pencils.shape)
    whitened = lax.all_to_all(whitened_rows, "bcol", split_axis=2, concat_axis=1, tiled=True)
    padded = extended(whitened, (("brow", 1), ("bcol", 2)), half_edge)
    col_freq = jnp.arange(pad_cols, dtype=jnp.int32)
    row_freq = jnp.arange(pad_rows, dtype=jnp.int32)
    depth_freq = jnp.arange(pad_depth, dtype=jnp.int32)
    depth_index = jnp.arange(depth_total, dtype=jnp.int32)
    tpl_index = jnp.arange(template_edge, dtype=jnp.int32)
    out_rows = jnp.arange(brick_rows, dtype=jnp.int32)
    out_cols = jnp.arange(brick_cols, dtype=jnp.int32)
    cos_cols, sin_cols = phase_tables(col_freq, col_freq, pad_cols)
    cos_rows, sin_rows = phase_tables(row_freq, row_freq, pad_rows)
    cos_depth, sin_depth = phase_tables(depth_freq, depth_index, pad_depth)
    tcos_cols, tsin_cols = phase_tables(tpl_index, col_freq, pad_cols)
    tcos_rows, tsin_rows = phase_tables(row_freq, tpl_index, pad_rows)
    tcos_depth, tsin_depth = phase_tables(depth_freq, tpl_index, pad_depth)
    back_depth_c, back_depth_s = phase_tables(depth_index - half_edge, depth_freq, pad_depth)
    back_rows_c, back_rows_s = phase_tables(out_rows, row_freq, pad_rows)
    back_cols_c, back_cols_s = phase_tables(col_freq, out_cols, pad_cols)
    box_rows = band_table(out_rows, row_freq, 0, template_edge)
    box_cols = band_table(out_cols, col_freq, 0, template_edge).T
    box_depth = band_table(depth_index, depth_index, -half_edge, half_edge)
    portion = lax.all_gather(padded, "orient", axis=0, tiled=True)
    col_real = jnp.einsum("nxy,yk->nxk", portion, cos_cols, precision=highest)
    col_imag = -jnp.einsum("nxy,yk->nxk", portion, sin_cols, precision=highest)
    spec_real = jnp.einsum("kx,nxy->nky", cos_rows, col_real, precision=highest) + jnp.einsum(
        "kx,nxy->nky", sin_rows, col_imag, precision=highest
    )
    spec_imag = jnp.einsum("kx,nxy->nky", cos_rows, col_imag, precision=highest) - jnp.einsum(
        "kx,nxy->nky", sin_rows, col_real, precision=highest
    )
    squares = portion * portion
    along_cols = jnp.einsum("nxy,yr->nxr", squares, box_cols, precision=highest)
    sum_real = jnp.einsum("kz,zxy->kxy", cos_depth, spec_real, precision=highest) + jnp.einsum(
        "kz,zxy->kxy", sin_depth, spec_imag, precision=highest
    )
    sum_imag = jnp.einsum("kz,zxy->kxy", cos_depth, spec_imag, precision=highest) - jnp.einsum(
        "kz,zxy->kxy", sin_depth, spec_real, precision=highest
    )
    sum_energy = jnp.einsum(
        "wz,zqr->wqr",
        box_depth,
        jnp.einsum("qx,nxr->nqr", box_rows, along_cols, precision=highest),
        precision=highest,
    )
    flattened = template.reshape(-1)
    centred = flattened - jnp.mean(flattened)
    normed = centred / jnp.sqrt(jnp.sum(centred * centred) + epsilon)
    voxel_total = flattened.shape[0]
    scaling = lax.rsqrt(sum_energy / voxel_total + epsilon)
    inverse_norm = 1.0 / (pad_depth * pad_rows * pad_cols)
    rotated = normed[voxel_maps[0]].reshape(template_edge, template_edge, template_edge)
    tcol_real = jnp.einsum("abc,ck->abk", rotated, tcos_cols, precision=highest)
    tcol_imag = -jnp.einsum("abc,ck->abk", rotated, tsin_cols, precision=highest)
    trow_real = jnp.einsum("kb,abc->akc", tcos_rows, tcol_real, precision=highest) + jnp.einsum(
        "kb,abc->akc", tsin_rows, tcol_imag, precision=highest
    )
    trow_imag = jnp.einsum("kb,abc->akc", tcos_rows, tcol_imag, precision=highest) - jnp.einsum(
        "kb,abc->akc", tsin_rows, tcol_real, precision=highest
    )
    tpl_real = jnp.einsum("ka,abc->kbc", tcos_depth, trow_real, precision=highest) + jnp.einsum(
        "ka,abc->kbc", tsin_depth, trow_imag, precision=highest
    )
    tpl_imag = jnp.einsum("ka,abc->kbc", tcos_depth, trow_imag, precision=highest) - jnp.einsum(
        "ka,abc->kbc", tsin_depth, trow_real, precision=highest
    )
    prod_real = sum_real * tpl_real + sum_imag * tpl_imag
    prod_imag = sum_imag * tpl_real - sum_real * tpl_imag
    depth_real = jnp.einsum("zk,kxy->zxy", back_depth_c, prod_real, precision=highest) - jnp.einsum(
        "zk,kxy->zxy", back_depth_s, prod_imag, precision=highest
    )
    depth_imag = jnp.einsum("zk,kxy->zxy", back_depth_c, prod_imag, precision=highest) + jnp.einsum(
        "zk,kxy->zxy", back_depth_s, prod_real, precision=highest
    )
    rows_real = jnp.einsum("qk,zky->zqy", back_rows_c, depth_real, precision=highest) - jnp.einsum(
        "qk,zky->zqy", back_rows_s, depth_imag, precision=highest
    )
    rows_imag = jnp.einsum("qk,zky->zqy", back_rows_c, depth_imag, precision=highest) + jnp.einsum(
        "qk,zky->zqy", back_rows_s, depth_real, precision=highest
    )
    correlation = jnp.einsum("zqk,kr->zqr", rows_real, back_cols_c, precision=highest) - jnp.einsum(
        "zqk,kr->zqr", rows_imag, back_cols_s, precision=highest
    )
    score = correlation * inverse_norm * scaling
    combined = lax.pmax(score, "orient")
    return lax.dynamic_slice_in_dim(
        combined, lax.axis_index("orient") * plane_count, plane_count, 0
    )


def solution(mesh):
    in_specs = (P("orient", "brow", "bcol"), P(), P("orient", None))
    out_specs = P("orient", "brow", "bcol")
    return jax.shard_map(shards, mesh=mesh, in_specs=in_specs, out_specs=out_specs, check_vma=False)
```

profile of v0, /device:TPU:2, one launch (start us, length us, event | category | flops | bytes accessed | tf_op | source)
XLA Modules:
  0.0 549.8 jit_solution(6854731164237918820)
XLA Ops:
  6.5 9.3 %all-to-all-start = ((f32[1,32,104]{2,0,1:T(1,128)}), f32[1,32,104]{2,0,1:T(1,128)S(1)}, u32[]{:S(2)}, u32[]{:S(2)}) async-start(f32[1,32,104]{2,0,1:T(1,128)} %bitcast.154), calls=%async_computation | async-start | bytes 32768 | tf_op jit(solution)/shard_map/all_to_all | solution.py:66
  15.8 1.6 reduce_sum.28
  18.1 1.6 multiply_reduce_fusion
  21.9 71.2 %gather_fusion = f32[13824]{0:T(1024)S(1)} fusion(f32[13824]{0:T(1024)S(1)} %div.38, s32[14336]{0:T(1024)S(1)} %pad_clamp_fusion), kind=kCustom, calls=%fused_computation | custom fusion | bytes 165888 | tf_op jit(solution)/shard_map/gather | solution.py:118
  96.6 1.5 fusion.61
  99.8 1.5 convolution_subtract_fusion.1
  101.5 13.9 %fusion.35 = f32[4,832]{1,0:T(4,128)S(1)} fusion(f32[4,832]{1,0:T(4,128)S(1)} %reshape.51), kind=kOutput, calls=%fused_computation.48 | convolution fusion | flops 39456768 | bytes 26624 | tf_op jit(solution)/shard_map/dot_general | solution.py:44
  115.3 14.1 %fusion.421 = (f32[4]{0:T(128)S(1)}, f32[4,832]{1,0:T(4,128)S(1)}, f32[832,4]{0,1:T(4,128)S(1)}) fusion(f32[4,832]{1,0:T(4,128)S(1)} %fusion.35, f32[4,832]{1,0:T(4,128)S(1)} %reshape.51), kind=kOutput, calls=%fused_computation.402 | convolution fusion | flops 39470076 | bytes 53264 | tf_op jit(solution)/shard_map/dot_general | solution.py:45
  129.7 14.1 %fusion.6 = f32[4,832]{1,0:T(4,128)S(1)} fusion(f32[4,832]{1,0:T(4,128)S(1)} %fusion.35, f32[4,832]{1,0:T(4,128)S(1)} %fusion.186), kind=kOutput, calls=%fused_computation.9 | convolution fusion | flops 39460096 | bytes 39936 | tf_op jit(solution)/shard_map/dot_general | solution.py:52
  143.8 13.7 %fusion.44 = f32[1,4,832]{2,1,0:T(4,128)S(1)} fusion(f32[4,832]{1,0:T(4,128)S(1)} %fusion.6, f32[4,832]{1,0:T(4,128)S(1)} %fusion.186, f32[832,4]{0,1:T(4,128)S(1)} %get-tuple-element.17), kind=kOutput, calls=%fused_computation.51 | convolution fusion | flops 39470080 | bytes 53248 | tf_op jit(solution)/shard_map/dot_general | solution.py:52
  158.8 1.7 reduce.4
  161.3 7.2 %all-to-all-start.1 = ((f32[8,1,416]{2,1,0:T(1,128)}), f32[8,1,416]{2,1,0:T(1,128)S(1)}, u32[]{:S(2)}, u32[]{:S(2)}) async-start(f32[8,1,416]{2,1,0:T(1,128)} %reshape.82), calls=%async_computation.1 | async-start | bytes 32768 | tf_op jit(solution)/shard_map/all_to_all | solution.py:68
  168.6 2.6 fusion.65
  171.2 3.6 all-to-all-done.1
  175.5 1.4 reshape.83
  178.1 1.3 collective-permute-start.1
  179.4 3.0 collective-permute-start
  182.4 2.7 convolution_add_fusion.1
  185.2 3.4 collective-permute-start.3
  188.6 3.9 collective-permute-start.2
  192.6 4.2 collective-permute-done.2
  196.9 71.5 %all_gather.3 = f32[32,56,128]{2,1,0:T(8,128)S(1)} all-gather(f32[1,56,128]{2,1,0:T(8,128)S(1)} %pad_maximum_fusion.1), channel_id=1, replica_groups=mesh['orient'=32,'brow'=2,'bcol'=8] {'orient'}, dimensions={0}, use_global_device_ids=true | all-gather | bytes 946176 | tf_op jit(solution)/shard_map/all_gather | solution.py:89
  274.3 1.5 fusion.55
  277.0 1.5 fusion.59
  278.5 1.5 convolution_subtract_fusion
  280.1 2.3 multiply_subtract_fusion
  285.7 1.2 fusion.53
  288.0 1.2 fusion.49
  289.3 1.2 fusion.32
  293.7 1.8 fusion.34
  295.6 245.6 %all-reduce.2.cloned.1.call-done = f32[32,32,104]{2,1,0:T(8,128)} async-done(((f32[32,32,104]{2,1,0:T(8,128)}), f32[32,32,104]{2,1,0:T(8,128)}) %all-reduce.2.cloned.1.call-update) | async-done | bytes 426000 | tf_op jit(solution)/shard_map/pmax | solution.py:151
  541.2 1.3 constant_dynamic-slice_fusion
  (54 shorter events, 25.5 us)
Async XLA Ops:
  6.5 15.1 %copy-start.2 = (s32[1,13824]{1,0:T(1,128)S(1)}, s32[1,13824]{1,0:T(1,128)}, u32[]{:S(2)}) copy-start(s32[1,13824]{1,0:T(1,128)} %param.5) | copy-start | bytes 165892
  6.5 94.8 %all-to-all-start = ((f32[1,32,104]{2,0,1:T(1,128)}), f32[1,32,104]{2,0,1:T(1,128)S(1)}, u32[]{:S(2)}, u32[]{:S(2)}) async-start(f32[1,32,104]{2,0,1:T(1,128)} %bitcast.154), calls=%async_computation | async-start | bytes 32768 | tf_op jit(solution)/shard_map/all_to_all | solution.py:66
  96.6 1.5 copy-start
  99.0 0.9 copy-start.1
  161.3 13.5 %all-to-all-start.1 = ((f32[8,1,416]{2,1,0:T(1,128)}), f32[8,1,416]{2,1,0:T(1,128)S(1)}, u32[]{:S(2)}, u32[]{:S(2)}) async-start(f32[8,1,416]{2,1,0:T(1,128)} %reshape.82), calls=%async_computation.1 | async-start | bytes 32768 | tf_op jit(solution)/shard_map/all_to_all | solution.py:68
  168.6 372.6 %all-reduce.2.cloned.1.call-start = ((), (), s32[]{:S(2)}) async-start(), calls=%async_computation.2 | async-start | bytes 1048576 | tf_op jit(solution)/shard_map/pmax | solution.py:151
  178.1 7.0 %collective-permute-start.1 = (f32[1,12,104]{2,1,0:T(8,128)S(1)}, f32[1,12,104]{2,1,0:T(8,128)S(1)}, u32[]{:S(2)}, u32[]{:S(2)}) collective-permute-start(f32[1,12,104]{2,1,0:T(8,128)S(1)} %get-tuple-element.12), channel_id=1, source_target_pairs={{8,0},{9,1},{10,2},{11,3},{12,4},{13,5},{14,6},{15,7},{24,16},{25,... | collective-permute-start | bytes 14984 | tf_op jit(solution)/shard_map/ppermute | solution.py:22
  179.4 5.7 %collective-permute-start = (f32[1,12,104]{2,1,0:T(8,128)S(1)}, f32[1,12,104]{2,1,0:T(8,128)S(1)}, u32[]{:S(2)}, u32[]{:S(2)}) collective-permute-start(f32[1,12,104]{2,1,0:T(8,128)S(1)} %get-tuple-element.11), channel_id=1, source_target_pairs={{0,8},{1,9},{2,10},{3,11},{4,12},{5,13},{6,14},{7,15},{16,24},{17,... | collective-permute-start | bytes 14984 | tf_op jit(solution)/shard_map/ppermute | solution.py:20
  185.2 7.4 %collective-permute-start.3 = (f32[1,56,12]{2,1,0:T(8,128)S(1)}, f32[1,56,12]{2,1,0:T(8,128)S(1)}, u32[]{:S(2)}, u32[]{:S(2)}) collective-permute-start(f32[1,56,12]{2,1,0:T(8,128)S(1)} %get-tuple-element.10), channel_id=1, source_target_pairs={{1,0},{2,1},{3,2},{4,3},{5,4},{6,5},{7,6},{9,8},{10,9},{11,10},{12... | collective-permute-start | bytes 8072 | tf_op jit(solution)/shard_map/ppermute | solution.py:22
  188.6 8.2 %collective-permute-start.2 = (f32[1,56,12]{2,1,0:T(8,128)S(1)}, f32[1,56,12]{2,1,0:T(8,128)S(1)}, u32[]{:S(2)}, u32[]{:S(2)}) collective-permute-start(f32[1,56,12]{2,1,0:T(8,128)S(1)} %get-tuple-element.9), channel_id=1, source_target_pairs={{0,1},{1,2},{2,3},{3,4},{4,5},{5,6},{6,7},{8,9},{9,10},{10,11},{11... | collective-permute-start | bytes 8072 | tf_op jit(solution)/shard_map/ppermute | solution.py:20
Sparse Core Ops, SparseCore 0:
  295.7 245.4 all-reduce.1
where the time goes:
time: 558 us; the launch traced here: 550 us
  waiting for transfers between devices  253 us (45%)
  matrix products  95.3 us (17%)
  local copies, waits for them, and re-layouts  78.7 us (14%)
  blocking collectives  71.5 us (13%)
  starting transfers between devices  28.2 us (5%)
  between operations  15.6 us (3%)
  other arithmetic  7.02 us (1%)
    pmax x1, waiting for transfers between devices, shards(): combined = lax.pmax(score, 'orient')  246 us
    all_gather x1, blocking collectives, shards(): portion = lax.all_gather(padded, 'orient', axis=0, tiled=True)  71.5 us
    gather x1, local copies, waits for them, and re-layouts, shards(): normed[voxel_maps[0]].reshape(template_edge, template_edge, template_edge)  71.2 us
    dot_general x1, matrix products, whiten_rows(): jnp.dot(spec_real * weights, cosine, precision=highest)  14.1 us
    dot_general x1, matrix products, whiten_rows(): spec_imag = -jnp.dot(rows_in, sine_table, precision=highest)  14.1 us
    dot_general x1, matrix products, whiten_rows(): spec_real = jnp.dot(rows_in, cosine, precision=highest)  13.9 us
    dot_general x1, matrix products, whiten_rows(): jnp.dot(spec_imag * weights, sine_table, precision=highest)  13.7 us
  transfers between devices with their start and end apart: 7, of which 3 were waited for; matrix products, arithmetic and copies ran while one was open for 16% of the time, Pallas kernels for 0%

commit v1 on v0

--- a/solution.py
+++ b/solution.py
@@ -86,7 +86,9 @@
     box_rows = band_table(out_rows, row_freq, 0, template_edge)
     box_cols = band_table(out_cols, col_freq, 0, template_edge).T
     box_depth = band_table(depth_index, depth_index, -half_edge, half_edge)
-    portion = lax.all_gather(padded, "orient", axis=0, tiled=True)
+    portion = jnp.concatenate(
+        lax.all_to_all(jnp.stack([padded] * lax.axis_size("orient")), "orient", 0, 0), axis=0
+    )
     col_real = jnp.einsum("nxy,yk->nxk", portion, cos_cols, precision=highest)
     col_imag = -jnp.einsum("nxy,yk->nxk", portion, sin_cols, precision=highest)
     spec_real = jnp.einsum("kx,nxy->nky", cos_rows, col_real, precision=highest) + jnp.einsum(

time: 558 us -> 512 us (0.918)
  blocking collectives: 71.5 us -> 25.4 us
  waiting for transfers between devices: 253 us -> 261 us
    all_gather x1 -> x0, blocking collectives: 71.5 us -> none  [shards(): portion = lax.all_gather(padded, 'orient', axis=0, tiled=True)]
    all_to_all x0 -> x2, blocking collectives: none -> 25.4 us  [the longest x1 15.4 us: shards(): lax.all_to_all(volume, 'bcol', split_axis=1, concat_axis=2, tiled=True)]
    pmax x1, waiting for transfers between devices: 246 us -> 256 us  [shards(): combined = lax.pmax(score, 'orient')]
    all_to_all x2 -> x1, starting transfers between devices: 16.5 us -> 14 us  [shards(): lax.all_to_all(jnp.stack([padded] * lax.axis_size('orient')), 'orient', 0...]
  transfers between devices with their start and end apart: 7 -> 6, of which waited for: 3 -> 3; matrix products, arithmetic and copies ran while one was open for 16% -> 17% of each run, Pallas kernels for 0% -> 0%
where the time goes in v1:
time: 512 us; the launch traced here: 503 us
  waiting for transfers between devices  261 us (51%)
  matrix products  94.1 us (18%)
  local copies, waits for them, and re-layouts  76.6 us (15%)
  starting transfers between devices  25.9 us (5%)
  blocking collectives  25.4 us (5%)
  between operations  15.7 us (3%)
    pmax x1, waiting for transfers between devices, shards(): combined = lax.pmax(score, 'orient')  256 us
    gather x1, local copies, waits for them, and re-layouts, shards(): normed[voxel_maps[0]].reshape(template_edge, template_edge, template_edge)  71.3 us
    all_to_all x1, blocking collectives, shards(): lax.all_to_all(volume, 'bcol', split_axis=1, concat_axis=2, tiled=True)  15.4 us
    dot_general x1, matrix products, whiten_rows(): spec_imag = -jnp.dot(rows_in, sine_table, precision=highest)  14.1 us
    all_to_all x1, starting transfers between devices, shards(): lax.all_to_all(jnp.stack([padded] * lax.axis_size('orient')), 'orient', 0...  14 us
    dot_general x1, matrix products, whiten_rows(): spec_real = jnp.dot(rows_in, cosine, precision=highest)  13.9 us
    dot_general x1, matrix products, whiten_rows(): jnp.dot(spec_imag * weights, sine_table, precision=highest)  13.7 us
    dot_general x1, matrix products, whiten_rows(): jnp.dot(spec_real * weights, cosine, precision=highest)  13.6 us
  transfers between devices with their start and end apart: 6, of which 3 were waited for; matrix products, arithmetic and copies ran while one was open for 17% of the time, Pallas kernels for 0%

profile of v1, /device:TPU:2, one launch (start us, length us, event | category | flops | bytes accessed | tf_op | source)
XLA Modules:
  0.0 502.6 jit_solution(7168008265487968231)
XLA Ops:
  6.5 15.4 %all_to_all.38 = f32[1,32,104]{2,0,1:T(1,128)S(1)} all-to-all(f32[1,32,104]{2,0,1:T(1,128)} %bitcast.161), channel_id=1, replica_groups=mesh['orient'=32,'brow'=2,'bcol'=8] {'bcol'}, dimensions={1} | all-to-all | bytes 26624 | tf_op jit(solution)/shard_map/all_to_all | solution.py:66
  22.0 13.9 %fusion.35 = f32[4,832]{1,0:T(4,128)S(1)} fusion(f32[4,832]{1,0:T(4,128)S(1)} %reshape.57), kind=kOutput, calls=%fused_computation.48 | convolution fusion | flops 39456768 | bytes 26624 | tf_op jit(solution)/shard_map/dot_general | solution.py:44
  35.9 14.1 %fusion.422 = (f32[4]{0:T(128)S(1)}, f32[4,832]{1,0:T(4,128)S(1)}, f32[832,4]{0,1:T(4,128)S(1)}) fusion(f32[4,832]{1,0:T(4,128)S(1)} %fusion.35, f32[4,832]{1,0:T(4,128)S(1)} %reshape.57), kind=kOutput, calls=%fused_computation.404 | convolution fusion | flops 39470076 | bytes 53264 | tf_op jit(solution)/shard_map/dot_general | solution.py:45
  50.2 13.6 %fusion.6 = f32[4,832]{1,0:T(4,128)S(1)} fusion(f32[4,832]{1,0:T(4,128)S(1)} %fusion.35, f32[4,832]{1,0:T(4,128)S(1)} %fusion.187), kind=kOutput, calls=%fused_computation.9 | convolution fusion | flops 39460096 | bytes 39936 | tf_op jit(solution)/shard_map/dot_general | solution.py:52
  63.9 13.7 %fusion.44 = f32[1,4,832]{2,1,0:T(4,128)S(1)} fusion(f32[4,832]{1,0:T(4,128)S(1)} %fusion.6, f32[4,832]{1,0:T(4,128)S(1)} %fusion.187, f32[832,4]{0,1:T(4,128)S(1)} %get-tuple-element.17), kind=kOutput, calls=%fused_computation.51 | convolution fusion | flops 39470080 | bytes 53248 | tf_op jit(solution)/shard_map/dot_general | solution.py:52
  78.8 1.7 reduce.4
  80.8 10.1 %all_to_all.39 = f32[8,1,416]{2,1,0:T(1,128)S(1)} all-to-all(f32[8,1,416]{2,1,0:T(1,128)S(1)} %reshape.89), channel_id=1, replica_groups=mesh['orient'=32,'brow'=2,'bcol'=8] {'bcol'}, dimensions={0} | all-to-all | bytes 26624 | tf_op jit(solution)/shard_map/all_to_all | solution.py:68
  92.4 1.4 collective-permute-start.1
  93.8 3.0 collective-permute-start
  97.8 3.4 collective-permute-start.3
  101.2 3.9 collective-permute-start.2
  105.1 4.2 collective-permute-done.2
  110.4 14.0 %all-to-all-start.2 = ((f32[32,1,56,128]{3,2,1,0:T(8,128)}), f32[32,1,56,128]{3,2,1,0:T(8,128)S(1)}, u32[]{:S(2)}, u32[]{:S(2)}) async-start(f32[32,1,56,128]{3,2,1,0:T(8,128)} %stack.2), calls=%async_computation.2 | async-start | bytes 1835008 | tf_op jit(solution)/shard_map/all_to_all | solution.py:90
  127.7 71.3 %gather_fusion = f32[13824]{0:T(1024)S(1)} fusion(f32[13824]{0:T(1024)S(1)} %div.38, s32[14336]{0:T(1024)S(1)} %pad_clamp_fusion), kind=kCustom, calls=%fused_computation | custom fusion | bytes 165888 | tf_op jit(solution)/shard_map/gather | solution.py:120
  203.4 1.5 fusion.63
  205.0 1.5 fusion.67
  206.5 1.6 convolution_subtract_fusion.1
  208.1 2.7 convolution_add_fusion.1
  210.8 1.1 convolution_negate_fusion
  214.1 1.2 fusion.109
  216.4 1.5 fusion.57
  219.0 1.5 fusion.61
  220.5 1.6 convolution_subtract_fusion
  222.2 2.1 multiply_subtract_fusion
  226.4 1.4 convolution_subtract_fusion.2
  227.8 1.2 fusion.55
  230.1 1.2 fusion.51
  231.4 1.2 fusion.32
  233.4 1.2 fusion.31
  236.4 1.9 fusion.34
  238.3 255.6 %all-reduce.2.cloned.1.call-done = f32[32,32,104]{2,1,0:T(8,128)} async-done(((f32[32,32,104]{2,1,0:T(8,128)}), f32[32,32,104]{2,1,0:T(8,128)}) %all-reduce.2.cloned.1.call-update) | async-done | bytes 426000 | tf_op jit(solution)/shard_map/pmax | solution.py:153
  493.9 1.3 constant_dynamic-slice_fusion
  (54 shorter events, 21.4 us)
Async XLA Ops:
  92.4 32.2 %copy-start.1 = (f32[24,24,24]{2,1,0:T(8,128)S(1)}, f32[24,24,24]{2,1,0:T(8,128)}, u32[]{:S(2)}) copy-start(f32[24,24,24]{2,1,0:T(8,128)} %param.4) | copy-start | bytes 165892
  92.4 4.5 collective-permute-start.1
  93.8 3.8 collective-permute-start
  97.8 7.4 %collective-permute-start.3 = (f32[1,56,12]{2,1,0:T(8,128)S(1)}, f32[1,56,12]{2,1,0:T(8,128)S(1)}, u32[]{:S(2)}, u32[]{:S(2)}) collective-permute-start(f32[1,56,12]{2,1,0:T(8,128)S(1)} %get-tuple-element.10), channel_id=1, source_target_pairs={{1,0},{2,1},{3,2},{4,3},{5,4},{6,5},{7,6},{9,8},{10,9},{11,10},{12... | collective-permute-start | bytes 8072 | tf_op jit(solution)/shard_map/ppermute | solution.py:22
  101.2 8.2 %collective-permute-start.2 = (f32[1,56,12]{2,1,0:T(8,128)S(1)}, f32[1,56,12]{2,1,0:T(8,128)S(1)}, u32[]{:S(2)}, u32[]{:S(2)}) collective-permute-start(f32[1,56,12]{2,1,0:T(8,128)S(1)} %get-tuple-element.9), channel_id=1, source_target_pairs={{0,1},{1,2},{2,3},{3,4},{4,5},{5,6},{6,7},{8,9},{9,10},{10,11},{11... | collective-permute-start | bytes 8072 | tf_op jit(solution)/shard_map/ppermute | solution.py:20
  110.4 17.0 %copy-start.2 = (s32[1,13824]{1,0:T(1,128)S(1)}, s32[1,13824]{1,0:T(1,128)}, u32[]{:S(2)}) copy-start(s32[1,13824]{1,0:T(1,128)} %param.5) | copy-start | bytes 165892
  110.4 100.3 %all-to-all-start.2 = ((f32[32,1,56,128]{3,2,1,0:T(8,128)}), f32[32,1,56,128]{3,2,1,0:T(8,128)S(1)}, u32[]{:S(2)}, u32[]{:S(2)}) async-start(f32[32,1,56,128]{3,2,1,0:T(8,128)} %stack.2), calls=%async_computation.2 | async-start | bytes 1835008 | tf_op jit(solution)/shard_map/all_to_all | solution.py:90
  124.5 369.5 %all-reduce.2.cloned.1.call-start = ((), (), s32[]{:S(2)}) async-start(), calls=%async_computation.3 | async-start | bytes 1048576 | tf_op jit(solution)/shard_map/pmax | solution.py:153
  220.5 1.6 copy-start
Sparse Core Ops, SparseCore 0:
  238.4 255.4 all-reduce.1
